TPU v7x, 32 devices: a whole 2x2x4 slice. The times are simulated.
32 devices in a mesh: grp: 2 (over y), ctx: 4 (over z), head: 2 (over x), sub: 2 (over core).
Axes of the slice: x: 2, y: 2, z: 4, core: 2. Of those that a mesh axis runs over, the one named last changes fastest.
Arguments:
- hidden: bfloat16 [8192, 4096], P(('grp', 'ctx', 'sub')), parts along dimension 0, may hold values from -6 to 6
- query_hidden: bfloat16 [512, 4096], P(('grp', 'ctx', 'sub')), parts along dimension 0, may hold values from -6 to 6
- norm_gain: float32 [4096], replicated, may hold values from 0.1 to 1.9
- w_query: bfloat16 [4096, 2048], P(None, 'head'), may hold values from -8 to 8
- w_key: bfloat16 [4096, 512], P(None, 'head'), may hold values from -1 to 1
- w_value: bfloat16 [4096, 512], P(None, 'head'), may hold values from -0.09375 to 0.09375
Outputs:
- context_out: bfloat16 [8192, 2048], P(('grp', 'ctx', 'sub'), 'head'), parts along dimension 0
- query_out: bfloat16 [512, 2048], P(('grp', 'ctx', 'sub'), 'head'), parts along dimension 0
There are 2 independent parts, one for each index of `grp`. A program takes and returns all parts, laid end to end along the dimension named above; an argument that names none is the same for every part. Nothing has to cross between parts.
All inputs are finite; a program needn't handle non-finite values.
Results may differ from a plain program's by a relative error of at most 0.018.
The roundings to bfloat16 on the way count: a program that leaves them out, or rounds other values in their place, can miss the bound.
Values may be sent and summed in bfloat16 or wider, within the bound.
A program may use at most 128 MiB of HBM per device.

v0:
```python
import jax
import jax.numpy as jnp
from jax import lax
from jax.sharding import PartitionSpec as P

HDIM = 128


rope_base = 500000.0
norm_eps = 1e-05
masked_score = -1e30


def from_root(value, axis, source):
    kept = jnp.where(lax.axis_index(axis) == source, value, 0).astype(value.dtype)
    return lax.psum(kept, axis)


def normalize(states, norm_gain):
    widened = states.astype(jnp.float32)
    meansq = jnp.mean(widened * widened, axis=-1, keepdims=True) + norm_eps
    return (widened * lax.rsqrt(meansq) * norm_gain).astype(jnp.bfloat16)


def rotate(tensor, positions):
    half_dim = tensor.shape[-1] // 2
    inverse = rope_base ** (-(jnp.arange(half_dim, dtype=jnp.float32) * 2.0 / tensor.shape[-1]))
    angles = positions.astype(jnp.float32)[:, None] * inverse[None, :]
    cosine = jnp.cos(angles)[:, None, :]
    sine_part = jnp.sin(angles)[:, None, :]
    lower_half = tensor[..., :half_dim]
    upper_half = tensor[..., half_dim:]
    return jnp.concatenate(
        [
            lower_half * cosine - upper_half * sine_part,
            upper_half * cosine + lower_half * sine_part,
        ],
        axis=-1,
    )


def project(normed, positions, w_query, w_key, w_value):
    row_count = normed.shape[0]
    query_heads = jnp.dot(normed, w_query, preferred_element_type=jnp.float32).reshape(
        row_count, -1, HDIM
    )
    key_heads = jnp.dot(normed, w_key, preferred_element_type=jnp.float32).reshape(
        row_count, -1, HDIM
    )
    value_heads = jnp.dot(normed, w_value, preferred_element_type=jnp.float32).reshape(
        row_count, -1, HDIM
    )
    return (
        rotate(query_heads, positions).astype(jnp.bfloat16),
        rotate(key_heads, positions).astype(jnp.bfloat16),
        value_heads.astype(jnp.bfloat16),
    )


def attend(query_heads, key_heads, value_heads, visible):
    row_count = query_heads.shape[0]
    head_count = query_heads.shape[1]
    kv_count = key_heads.shape[1]
    grouped = query_heads.reshape(row_count, kv_count, head_count // kv_count, HDIM)
    scores = jnp.einsum(
        "nkgd,mkd->nkgm", grouped, key_heads, preferred_element_type=jnp.float32
    ) * HDIM ** (-0.5)
    mask_full = visible[:, None, None, :]
    scores = jnp.where(mask_full, scores, masked_score)
    maxima = jnp.max(scores, axis=-1)
    weights = jnp.where(mask_full, jnp.exp(scores - maxima[..., None]), 0.0)
    totals = jnp.sum(weights, axis=-1)
    accumulated = jnp.einsum(
        "nkgm,mkd->nkgd",
        weights.astype(jnp.bfloat16),
        value_heads,
        preferred_element_type=jnp.float32,
    )
    return (
        maxima.reshape(row_count, head_count),
        totals.reshape(row_count, head_count),
        accumulated.reshape(row_count, head_count, HDIM),
    )


def shards(hidden, query_hidden, norm_gain, w_query, w_key, w_value):
    row_count = hidden.shape[0]
    ctx_index = lax.axis_index("ctx")
    sub_index = lax.axis_index("sub")
    sub_count = lax.axis_size("sub")
    ctx_count = lax.axis_size("ctx")
    block_len = row_count * sub_count
    positions = (
        ctx_index * block_len + sub_index * row_count + jnp.arange(row_count, dtype=jnp.int32)
    )
    queries, key_rows, value_rows = project(
        normalize(hidden, norm_gain), positions, w_query, w_key, w_value
    )
    own_pair = jnp.stack([key_rows, value_rows])
    block_pair = lax.all_gather(own_pair, "sub", axis=1, tiled=True)
    anchor_pair = from_root(block_pair, "ctx", 0)
    key_positions = ctx_index * block_len + jnp.arange(block_len, dtype=jnp.int32)
    visible = jnp.concatenate(
        [
            jnp.broadcast_to(ctx_index > 0, (row_count, block_len)),
            positions[:, None] >= key_positions[None, :],
        ],
        axis=1,
    )
    all_keys = jnp.concatenate([anchor_pair[0], block_pair[0]], axis=0)
    all_values = jnp.concatenate([anchor_pair[1], block_pair[1]], axis=0)
    maxima, totals, accumulated = attend(queries, all_keys, all_values, visible)
    context_out = (accumulated / totals[..., None]).astype(jnp.bfloat16).reshape(row_count, -1)
    query_count = query_hidden.shape[0]
    device_slot = ctx_index * sub_count + sub_index
    context_len = ctx_count * block_len
    query_positions = (
        context_len + device_slot * query_count + jnp.arange(query_count, dtype=jnp.int32)
    )
    own_queries, own_qkeys, own_qvalues = project(
        normalize(query_hidden, norm_gain), query_positions, w_query, w_key, w_value
    )
    every_query = lax.all_gather(own_queries, ("ctx", "sub"), axis=0, tiled=True)
    query_total = every_query.shape[0]
    every_position = context_len + jnp.arange(query_total, dtype=jnp.int32)
    near_keys = jnp.concatenate([key_rows, own_qkeys], axis=0)
    near_values = jnp.concatenate([value_rows, own_qvalues], axis=0)
    seen = jnp.concatenate(
        [
            jnp.ones((query_total, row_count), dtype=bool),
            every_position[:, None] >= query_positions[None, :],
        ],
        axis=1,
    )
    row_maxima, row_totals, row_sums = attend(every_query, near_keys, near_values, seen)
    global_max = lax.pmax(row_maxima, ("ctx", "sub"))
    factor = jnp.exp(row_maxima - global_max)
    totals_mine, sums_mine = (
        lax.psum_scatter(
            (row_totals * factor).astype(jnp.bfloat16),
            ("ctx", "sub"),
            scatter_dimension=0,
            tiled=True,
        ).astype(jnp.float32),
        lax.psum_scatter(
            (row_sums * factor[..., None]).astype(jnp.bfloat16),
            ("ctx", "sub"),
            scatter_dimension=0,
            tiled=True,
        ).astype(jnp.float32),
    )
    query_out = (sums_mine / totals_mine[..., None]).astype(jnp.bfloat16).reshape(query_count, -1)
    return (context_out, query_out)


def solution(mesh):
    return jax.shard_map(
        shards,
        mesh=mesh,
        in_specs=(
            P(("grp", "ctx", "sub"), None),
            P(("grp", "ctx", "sub"), None),
            P(),
            P(None, "head"),
            P(None, "head"),
            P(None, "head"),
        ),
        out_specs=(P(("grp", "ctx", "sub"), "head"), P(("grp", "ctx", "sub"), "head")),
        check_vma=False,
    )
```

profile of v0, /device:TPU:31, one launch (start us, length us, event | category | flops | bytes accessed | tf_op | source)
XLA Modules:
  0.0 191.4 jit_solution(15634020181294040750)
XLA Ops:
  8.1 3.2 %fusion.7 = f32[512]{0:T(512)S(1)} fusion(bf16[512,4096]{1,0:T(8,128)(2,1)} %param.6), kind=kLoop, calls=%fused_computation.11 | loop fusion | flops 6290944 | bytes 4196352 | tf_op jit(solution)/shard_map/reduce_sum | solution.py:21
  11.3 4.5 %convolution_convert_fusion = bf16[512,256]{0,1:T(8,128)(2,1)S(1)} fusion(bf16[4096,256]{1,0:T(8,128)(2,1)} %param.11, bf16[512,4096]{1,0:T(8,128)(2,1)} %param.6, f32[4096]{0:T(1024)} %param.8, f32[512]{0:T(512)S(1)} %add_rsqrt_fusion), kind=kOutput, calls=%fused_computation.27 | convolution fusion | flops 1082261504 | bytes 6572032 | tf_op jit(solution)/shard_map/dot_general | solution.py:50
  15.8 0.8 copy.37
  16.7 3.8 %fusion.55 = f32[512,256]{0,1:T(8,128)S(1)} fusion(bf16[4096,256]{1,0:T(8,128)(2,1)S(1)} %copy-done, bf16[512,4096]{1,0:T(8,128)(2,1)} %param.6, f32[4096]{0:T(1024)S(1)} %copy-done.11, f32[512]{0:T(512)S(1)} %add_rsqrt_fusion), kind=kOutput, calls=%fused_computation.98 | convolution fusion | flops 1082130432 | bytes 6834176 | tf_op jit(solution)/shard_map/dot_general | solution.py:47
  20.7 1.0 copy.61
  21.7 1.0 multiply_cosine_fusion
  22.7 1.2 subtract_convert_fusion.1
  24.7 1.9 pad_maximum_fusion.1
  27.7 5.0 %convolution_bitcast_fusion.1 = f32[4,8,8,128]{3,1,2,0:T(8,128)S(1)} fusion(bf16[4096,1024]{1,0:T(8,128)(2,1)} %param.9, bf16[32,4096]{1,0:T(8,128)(2,1)S(1)} %copy-done.3, f32[4096]{0:T(1024)S(1)} %copy-done.11, f32[32]{0:T(128)S(1)} %add_rsqrt_fusion.1), kind=kOutput, calls=%fused_computation.28 | convolution fusion | flops 268959744 | bytes 8798336 | tf_op jit(solution)/shard_map/dot_general | solution.py:44
  32.9 15.4 %all_gather.7 = bf16[256,8,128]{2,1,0:T(8,128)(2,1)S(1)} all-gather(bf16[32,8,128]{2,1,0:T(8,128)(2,1)S(1)} %pad_maximum_fusion.6), channel_id=1, replica_groups=mesh['grp'=2,'ctx'=4,'head'=2,'sub'=2] {'ctx','sub'}, dimensions={0}, use_global_device_ids=true | all-gather | bytes 589824 | tf_op jit(solution)/shard_map/all_gather | solution.py:123
  48.6 3.0 %fusion.10 = (f32[256,2,4]{0,2,1:T(4,128)S(1)}, f32[2,544,256,4]{2,1,3,0:T(8,128)}) fusion(pred[256,544]{0,1:T(8,128)(4,1)S(1)} %concatenate.63, bf16[256,2,4,128]{3,0,2,1:T(8,128)(2,1)S(1)} %bitcast.121, bf16[32,2,64]{2,0,1:T(8,128)(2,1)S(1)} %get-tuple-element.17, bf16[32,2,64]{2,0,1:T(8,128)(2,1)S(1)} %get-tuple-element.16, ...), kind=kOutput, calls=%fused_computation.16 | convolution fusion | flops 289667072 | bytes 5406720 | tf_op jit(solution)/shard_map/nkgd,mkd->nkgm/dot_general | solution.py:65
  51.6 3.4 %fusion.13 = f32[256,2,4]{0,2,1:T(4,128)S(1)} fusion(f32[2,544,256,4]{2,1,3,0:T(8,128)} %get-tuple-element.27, f32[256,2,4]{0,2,1:T(4,128)S(1)} %get-tuple-element.26, pred[256,544]{0,1:T(8,128)(4,1)S(1)} %concatenate.63), kind=kLoop, calls=%fused_computation.18 | loop fusion | flops 5568512 | bytes 4612096 | tf_op jit(solution)/shard_map/reduce_sum | solution.py:72
  55.0 13.3 %pmax.7 = f32[256,8]{0,1:T(8,128)S(1)} all-reduce(f32[256,8]{0,1:T(8,128)S(1)} %reshape.243), channel_id=1, replica_groups=mesh['grp'=2,'ctx'=4,'head'=2,'sub'=2] {'ctx','sub'}, use_global_device_ids=true, to_apply=%region_6.7 | all-reduce | flops 2048 | bytes 16384 | tf_op jit(solution)/shard_map/pmax | solution.py:136
  68.3 0.7 copy.59
  70.0 3.6 %fusion.15 = f32[2,128,256,4]{2,1,3,0:T(8,128)S(1)} fusion(f32[2,544,256,4]{2,1,3,0:T(8,128)} %get-tuple-element.27, f32[256,2,4]{0,2,1:T(4,128)S(1)} %get-tuple-element.26, pred[256,544]{0,1:T(8,128)(4,1)S(1)} %concatenate.63, bf16[32,2,128]{2,0,1:T(8,128)(2,1)S(1)} %bitcast.125, bf16[512,2,128]{2,0,1:T(8,128)(2,1)S(1)} %copy.44), kind=kOutput, calls=%fused_computation.20 | convolution fusion | flops 291340288 | bytes 5931008 | tf_op jit(solution)/shard_map/nkgm,mkd->nkgd/dot_general | solution.py:73
  74.1 1.2 multiply_convert_fusion
  75.3 10.6 %convolution_bitcast_fusion = f32[64,8,8,128]{3,1,2,0:T(8,128)} fusion(bf16[4096,1024]{1,0:T(8,128)(2,1)} %param.9, bf16[512,4096]{1,0:T(8,128)(2,1)} %param.6, f32[4096]{0:T(1024)S(1)} %copy-done.11, f32[512]{0:T(512)S(1)} %add_rsqrt_fusion), kind=kOutput, calls=%fused_computation.26 | convolution fusion | flops 4303355904 | bytes 14698496 | tf_op jit(solution)/shard_map/dot_general | solution.py:44
  85.9 2.1 %copy.66 = f32[64,8,8,128]{3,2,1,0:T(8,128)S(1)} copy(f32[64,8,8,128]{3,1,2,0:T(8,128)} %convolution_bitcast_fusion) | data formatting | bytes 4194304
  88.0 1.1 broadcast_select_fusion
  89.1 0.7 subtract_convert_fusion
  90.0 1.1 copy.39
  91.6 1.3 concatenate.57
  92.8 5.4 %reduce-scatter.7.cloned.1.call-done = bf16[32,8]{1,0:T(8,128)(2,1)} async-done(((bf16[256,8]{1,0:T(8,128)(2,1)}), bf16[32,8]{1,0:T(8,128)(2,1)}) %reduce-scatter.7.cloned.1.call-update) | async-done | bytes 528
  98.2 0.8 copy.60
  99.1 43.9 %reduce-scatter.5.cloned.1.call-done = bf16[32,8,128]{2,1,0:T(8,128)(2,1)} async-done(((bf16[256,8,128]{2,1,0:T(8,128)(2,1)}), bf16[32,8,128]{2,1,0:T(8,128)(2,1)}) %reduce-scatter.5.cloned.1.call-update) | async-done | bytes 65552 | tf_op jit(solution)/shard_map/reduce_scatter | solution.py:145
  143.0 0.9 divide_convert_fusion
  144.6 0.9 slice_bitcast_fusion.2
  145.5 1.3 slice_bitcast_fusion.3
  146.8 20.6 %fusion.59 = (f32[512,2,4]{0,2,1:T(4,128)S(1)}, bf16[512,2,4,2048]{0,3,2,1:T(8,128)(2,1)}) fusion(pred[512,2048]{0,1:T(8,128)(4,1)} %concatenate.57, bf16[1024,2,128]{2,0,1:T(8,128)(2,1)} %get-tuple-element.11, bf16[1024,2,128]{2,0,1:T(8,128)(2,1)S(1)} %get-tuple-element.9, bf16[512,2,4,64]{3,0,2,1:T(8,128)(2,1)} %bitcast.115, ...), kind=kOutput, calls=%fused_computation.101 | convolution fusion | flops 2202011648 | bytes 19939328 | tf_op jit(solution)/shard_map/sub | solution.py:71
  167.5 9.5 %fusion.2 = f32[2,128,512,4]{2,1,3,0:T(8,128)} fusion(bf16[512,2,4,2048]{0,3,2,1:T(8,128)(2,1)} %get-tuple-element.25, bf16[1024,2,128]{2,0,1:T(8,128)(2,1)S(1)} %get-tuple-element.10, bf16[1024,2,128]{2,0,1:T(8,128)(2,1)S(1)} %get-tuple-element.8), kind=kOutput, calls=%fused_computation.4 | convolution fusion | flops 2149580800 | bytes 19922944 | tf_op jit(solution)/shard_map/nkgm,mkd->nkgd/dot_general | solution.py:73
  177.1 3.1 %copy.43 = f32[512,1024]{1,0:T(8,128)} copy(f32[512,1024]{0,1:T(8,128)} %bitcast.111) | data formatting | bytes 4194304 | tf_op jit(solution)/shard_map/reshape | solution.py:82
  180.8 3.2 %fusion.18 = bf16[512,1024]{1,0:T(8,128)(2,1)} fusion(f32[512,1024]{1,0:T(8,128)} %copy.43, f32[64,8,8,128]{3,2,1,0:T(8,128)S(1)} %bitcast.112), kind=kLoop, calls=%fused_computation.23 | loop fusion | flops 1048576 | bytes 5242880 | tf_op jit(solution)/shard_map/convert_element_type | solution.py:113
  (70 shorter events, 6.1 us)
Async XLA Ops:
  8.0 8.7 %copy-start = (bf16[4096,256]{1,0:T(8,128)(2,1)S(1)}, bf16[4096,256]{1,0:T(8,128)(2,1)}, u32[]{:S(2)}) copy-start(bf16[4096,256]{1,0:T(8,128)(2,1)} %param.10) | copy-start | bytes 6291460
  8.0 80.0 %all-gather.2.cloned.1.call-start = ((), (), s32[]{:S(2)}) async-start(), calls=%async_computation.2 | async-start | bytes 1572864 | tf_op jit(solution)/shard_map/all_gather | solution.py:100
  11.3 5.3 %copy-start.11 = (f32[4096]{0:T(1024)S(1)}, f32[4096]{0:T(1024)}, u32[]{:S(2)}) copy-start(f32[4096]{0:T(1024)} %param.8) | copy-start | bytes 49156
  15.8 0.9 copy-start.5
  20.4 6.2 %copy-start.3 = (bf16[32,4096]{1,0:T(8,128)(2,1)S(1)}, bf16[32,4096]{1,0:T(8,128)(2,1)}, u32[]{:S(2)}) copy-start(bf16[32,4096]{1,0:T(8,128)(2,1)} %param.7) | copy-start | bytes 786436
  23.9 0.7 copy-start.7
  23.9 0.8 copy-start.9
  26.6 71.7 %reduce-scatter.7.cloned.1.call-start = ((), (), s32[]{:S(2)}) async-start(), calls=%async_computation.5 | async-start | bytes 73728
  27.6 20.9 %copy-start.8 = (bf16[512,2,64]{2,0,1:T(8,128)(2,1)S(1)}, bf16[512,2,64]{2,0,1:T(8,128)(2,1)}, u32[]{:S(2)}) copy-start(bf16[512,2,64]{2,0,1:T(8,128)(2,1)} %copy-done.7) | copy-start | bytes 393220
  27.6 20.9 %copy-start.10 = (bf16[512,2,64]{2,0,1:T(8,128)(2,1)S(1)}, bf16[512,2,64]{2,0,1:T(8,128)(2,1)}, u32[]{:S(2)}) copy-start(bf16[512,2,64]{2,0,1:T(8,128)(2,1)} %copy-done.9) | copy-start | bytes 393220
  48.6 20.7 %copy-start.4 = (bf16[4096,256]{1,0:T(8,128)(2,1)S(1)}, bf16[4096,256]{1,0:T(8,128)(2,1)}, u32[]{:S(2)}) copy-start(bf16[4096,256]{1,0:T(8,128)(2,1)} %param.11) | copy-start | bytes 6291460
  51.6 18.2 %copy-start.6 = (bf16[512,256]{0,1:T(8,128)(2,1)S(1)}, bf16[512,256]{0,1:T(8,128)(2,1)}, u32[]{:S(2)}) copy-start(bf16[512,256]{0,1:T(8,128)(2,1)} %copy-done.5) | copy-start | bytes 786436
  69.1 74.0 %reduce-scatter.5.cloned.1.call-start = ((), (), s32[]{:S(2)}) async-start(), calls=%async_computation.4 | async-start | bytes 589824 | tf_op jit(solution)/shard_map/reduce_scatter | solution.py:145
  75.3 70.2 %all-reduce.4.cloned.1.call-start = ((), (), s32[]{:S(2)}) async-start(), calls=%async_computation.3 | async-start | bytes 2097152 | tf_op jit(solution)/shard_map/psum | solution.py:16
  89.9 54.7 %copy-start.2 = (bf16[2,1024,2,128]{3,1,2,0:T(8,128)(2,1)S(1)}, bf16[2,1024,2,128]{3,1,2,0:T(8,128)(2,1)}, u32[]{:S(2)}) copy-start(bf16[2,1024,2,128]{3,1,2,0:T(8,128)(2,1)} %all-gather.2.cloned.1.call-done) | copy-start | bytes 3145732
  177.1 6.9 %copy-start.1 = (bf16[4096,256]{1,0:T(8,128)(2,1)S(1)}, bf16[4096,256]{1,0:T(8,128)(2,1)}, u32[]{:S(2)}) copy-start(bf16[4096,256]{1,0:T(8,128)(2,1)} %param.10) | copy-start | bytes 6291460
Sparse Core Ops, SparseCore 0:
  26.7 10.6 all-gather.1
  89.3 55.5 all-reduce.3
Sparse Core Ops, SparseCore 1:
  69.1 29.0 reduce-scatter.6
  100.4 42.6 reduce-scatter.4
where the time goes:
time: 194 us; the launch traced here: 191 us
  matrix products  61.5 us (32%)
  waiting for transfers between devices  49.4 us (25%)
  blocking collectives  28.7 us (15%)
  other arithmetic  18.8 us (10%)
  local copies, waits for them, and re-layouts  16.7 us (9%)
  between operations  15.9 us (8%)
    reduce_scatter x1, waiting for transfers between devices, shards(): lax.psum_scatter((row_sums * factor[..., None]).astype(jnp.bfloat16), ('c...  43.9 us
    sub x1, matrix products, attend(): weights = jnp.where(mask_full, jnp.exp(scores - maxima[..., None]), 0.0)  20.6 us
    dot_general x2, matrix products, project(): jnp.dot(normed, w_query, preferred_element_type=jnp.float32)  15.6 us
    all_gather x1, blocking collectives, shards(): lax.all_gather(own_queries, ('ctx', 'sub'), axis=0, tiled=True)  15.4 us
    pmax x1, blocking collectives, shards(): global_max = lax.pmax(row_maxima, ('ctx', 'sub'))  13.3 us
    dot_general x2, matrix products, attend(): jnp.einsum('nkgm,mkd->nkgd', weights.astype(jnp.bfloat16), value_heads, p...  13.1 us
    unnamed x31, local copies, waits for them, and re-layouts  6.27 us
    unnamed x5, waiting for transfers between devices  5.48 us
  transfers between devices with their start and end apart: 4, of which 2 were waited for; matrix products, arithmetic and copies ran while one was open for 21% of the time, Pallas kernels for 0%

commit v1 on v0

v1 whole, which is shorter than its diff:
```python
import functools
import math

import jax
import jax.numpy as jnp
from jax import lax
from jax.experimental import pallas as pl
from jax.experimental.pallas import tpu as pltpu
from jax.sharding import PartitionSpec as P

HDIM = 128
TILE = 128
CHUNKS = 4

rope_base = 500000.0
norm_eps = 1e-05
masked_score = -1e30
exponent_scale = HDIM ** (-0.5) * math.log2(math.e)

MESH = pl.DeviceIdType.MESH
NT_DIMS = (((1,), (1,)), ((), ()))


def kernel(
    sizes,
    hidden_hbm, qhidden_hbm, gain_ref, cos_ref, sin_ref, wq_hbm, wk_hbm, wv_hbm,
    out_ref, qout_ref,
    hid, qhid, normed, wq, wk, wv, heads_q, own_q, all_q, blk, qkv, anc,
    acc1, max1, sacc, sstat, racc, rstat,
    load_sem, qload_sem, wk_sem, wv_sem, wq_sem,
    blk_sem, qkv_sem, chain_send, chain_recv, pair_send, pair_recv,
    q_send, q_recv, r_send, r_recv, t_send, t_recv,
):
    ctx_count, sub_count, query_rows = sizes
    rows, width = hid.shape
    padded = qhid.shape[0]
    q_heads = heads_q.shape[0]
    key_cols = wk.shape[1]
    kv_heads = key_cols // HDIM
    group = q_heads // kv_heads
    tiles = rows // TILE
    part = rows // CHUNKS
    ctx = lax.axis_index("ctx")
    sub = lax.axis_index("sub")
    peer = lax.rem(sub + 1, sub_count)

    def load_rows(i):
        piece = pl.ds(i * TILE, TILE)
        return pltpu.make_async_copy(hidden_hbm.at[piece], hid.at[piece], load_sem.at[i])

    wq_width = wq.shape[2]
    wq_tiles = wq.shape[0]

    def load_wq(j):
        return pltpu.make_async_copy(
            wq_hbm.at[:, pl.ds(j * wq_width, wq_width)], wq.at[j], wq_sem.at[j]
        )

    load_query = pltpu.make_async_copy(qhidden_hbm, qhid, qload_sem)
    load_wk = pltpu.make_async_copy(wk_hbm, wk, wk_sem)
    load_wv = pltpu.make_async_copy(wv_hbm, wv, wv_sem)
    for i in range(tiles):
        load_rows(i).start()
    load_query.start()
    load_wk.start()
    load_wv.start()
    for j in range(wq_tiles):
        load_wq(j).start()

    barrier = pltpu.get_barrier_semaphore()
    for step in range(1, ctx_count):
        other = lax.rem(ctx + step, ctx_count)
        pl.semaphore_signal(barrier, inc=1, device_id={"ctx": other}, device_id_type=MESH)
    pl.semaphore_signal(barrier, inc=1, device_id={"sub": peer}, device_id_type=MESH)

    gain = gain_ref[...]

    def norm_rows(source, start, target, count):
        wide = source[pl.ds(start, count), :].astype(jnp.float32)
        meansq = jnp.mean(wide * wide, axis=-1, keepdims=True) + norm_eps
        normed[pl.ds(target, count), :] = (wide * lax.rsqrt(meansq) * gain).astype(jnp.bfloat16)

    for i in range(tiles):
        load_rows(i).wait()

        @pl.loop(0, TILE // 16)
        def _(b):
            start = pl.multiple_of(i * TILE + b * 16, 16)
            norm_rows(hid, start, start, 16)

    load_query.wait()
    for b in range(padded // 16):
        norm_rows(qhid, b * 16, rows + b * 16, 16)

    def rotated(values, head):
        cols = values[:, head * HDIM:(head + 1) * HDIM]
        return (cols * cos_ref[...] + pltpu.roll(cols, HDIM // 2, 1) * sin_ref[...]).astype(
            jnp.bfloat16
        )

    load_wk.wait()
    keys = jnp.dot(normed[...], wk[...], preferred_element_type=jnp.float32)
    for h in range(kv_heads):
        turned = rotated(keys, h)
        blk[sub, :, pl.ds(h * HDIM, HDIM)] = turned[:rows]
        qkv[sub, :, pl.ds(h * HDIM, HDIM)] = turned[rows:]
    load_wv.wait()
    values = jnp.dot(normed[...], wv[...], preferred_element_type=jnp.float32).astype(jnp.bfloat16)
    blk[sub, :, pl.ds(key_cols, key_cols)] = values[:rows]
    qkv[sub, :, pl.ds(key_cols, key_cols)] = values[rows:]

    pl.semaphore_wait(barrier, ctx_count)

    below = lax.rem(ctx + 1, ctx_count)

    def send_first(i):
        return pltpu.make_async_remote_copy(
            blk.at[sub, pl.ds(i * part, part)], anc.at[sub, i],
            chain_send.at[i], chain_recv.at[i],
            device_id={"ctx": below}, device_id_type=MESH,
        )

    def send_on(i):
        return pltpu.make_async_remote_copy(
            anc.at[sub, i], anc.at[sub, i],
            chain_send.at[i], chain_recv.at[i],
            device_id={"ctx": below}, device_id_type=MESH,
        )

    def send_pair(i):
        return pltpu.make_async_remote_copy(
            anc.at[sub, i], anc.at[sub, i],
            pair_send.at[i], pair_recv.at[i],
            device_id={"sub": peer}, device_id_type=MESH,
        )

    def recv_pair(i):
        return pltpu.make_async_remote_copy(
            anc.at[peer, i], anc.at[peer, i],
            pair_send.at[i], pair_recv.at[i],
            device_id={"sub": peer}, device_id_type=MESH,
        )

    @pl.when(ctx == 0)
    def _():
        for i in range(CHUNKS):
            send_first(i).start()

    def swap(ref, sems, place):
        return pltpu.make_async_remote_copy(
            ref.at[place], ref.at[place], sems.at[0], sems.at[1],
            device_id={"sub": peer}, device_id_type=MESH,
        )

    swap(blk, blk_sem, sub).start()
    swap(qkv, qkv_sem, sub).start()

    def forward(i, which):
        @pl.when(which)
        def _():
            send_on(i).wait_recv()

            @pl.when(ctx < ctx_count - 1)
            def _():
                send_on(i).start()

            send_pair(i).start()

    per_tile = wq_width // HDIM
    for j in range(wq_tiles):
        load_wq(j).wait()

        made = jnp.dot(normed[...], wq[j], preferred_element_type=jnp.float32)
        for t in range(per_tile):
            turned = rotated(made, t)
            heads_q[j * per_tile + t] = turned[:rows]
            own_q[j * per_tile + t] = turned[rows:]

    def send_query(step):
        other = lax.rem(ctx + step, ctx_count)
        return pltpu.make_async_remote_copy(
            own_q, all_q.at[ctx], q_send.at[other], q_recv.at[ctx],
            device_id={"ctx": other}, device_id_type=MESH,
        )

    def recv_query(step):
        other = lax.rem(ctx + step, ctx_count)
        return pltpu.make_async_remote_copy(
            own_q, all_q.at[other], q_send.at[other], q_recv.at[other],
            device_id={"ctx": other}, device_id_type=MESH,
        )

    for step in range(1, ctx_count):
        send_query(step).start()
    all_q[ctx] = own_q[...]

    forward(0, ctx == 1)

    def scores_of(q, k):
        return lax.dot_general(q, k, NT_DIMS, preferred_element_type=jnp.float32)

    def weights_of(s, m):
        return jnp.exp2((s - m) * exponent_scale).astype(jnp.bfloat16)

    def with_ones(v):
        return jnp.concatenate([v, jnp.ones_like(v)], axis=1)

    def add_up(p, v):
        return jnp.dot(p, with_ones(v), preferred_element_type=jnp.float32)

    def kcols(kh):
        return slice(kh * HDIM, (kh + 1) * HDIM)

    def vcols(kh):
        return slice(key_cols + kh * HDIM, key_cols + (kh + 1) * HDIM)

    def tile_q(kh, start):
        return heads_q[kh * group:(kh + 1) * group, pl.ds(start, TILE), :].reshape(
            group * TILE, HDIM
        )

    for t in range(tiles):
        span = (t + 1) * TILE
        for kh in range(kv_heads):
            s = scores_of(tile_q(kh, t * TILE), blk[sub, :span, kcols(kh)])
            row = lax.broadcasted_iota(jnp.int32, (TILE, span), 0) + t * TILE
            col = lax.broadcasted_iota(jnp.int32, (TILE, span), 1)
            s = jnp.where(
                (row >= col)[None], s.reshape(group, TILE, span), masked_score
            ).reshape(group * TILE, span)
            m = jnp.max(s, axis=-1, keepdims=True)
            acc1[kh, t] = add_up(weights_of(s, m), blk[sub, :span, vcols(kh)])
            max1[kh, t] = jnp.broadcast_to(m, (group * TILE, HDIM))
        if t == tiles // 2 - 1:
            forward(1, ctx == 1)

    forward(2, ctx == 1)
    forward(0, ctx == 2)

    def merged(kh, t, k, v):
        s = scores_of(tile_q(kh, pl.multiple_of(t * TILE, TILE)), k)
        before = max1[kh, t]
        m = jnp.maximum(jnp.max(s, axis=-1, keepdims=True), before)
        factor = jnp.exp2((before - m) * exponent_scale)
        acc = acc1[kh, t] * jnp.concatenate([factor, factor], axis=1)
        return m, acc + add_up(weights_of(s, m[:, :1]), v)

    swap(blk, blk_sem, peer).wait_recv()
    swap(qkv, qkv_sem, peer).wait_recv()

    @pl.when(sub > 0)
    def _():
        @pl.loop(0, tiles)
        def _(t):
            for kh in range(kv_heads):
                m, acc = merged(kh, t, blk[0, :, kcols(kh)], blk[0, :, vcols(kh)])
                acc1[kh, t] = acc
                max1[kh, t] = m

    forward(3, ctx == 1)
    forward(1, ctx == 2)

    for step in range(1, ctx_count):
        recv_query(step).wait_recv()

    total = ctx_count * group * padded
    keys_q = sub_count * padded
    shape4 = (ctx_count, group, padded, keys_q)
    owner = lax.broadcasted_iota(jnp.int32, shape4, 0)
    place = lax.broadcasted_iota(jnp.int32, shape4, 2)
    key_at = lax.broadcasted_iota(jnp.int32, shape4, 3)
    query_pos = (owner * sub_count + sub) * query_rows + place
    key_sub = jnp.where(key_at >= padded, 1, 0)
    key_row = key_at - key_sub * padded
    key_pos = (ctx * sub_count + key_sub) * query_rows + key_row
    seen = (query_pos >= key_pos) & (key_row < query_rows)
    lane = lax.broadcasted_iota(jnp.int32, (padded, HDIM), 1)
    stats = [jnp.zeros((padded, HDIM), jnp.float32) for _ in range(ctx_count)]
    for kh in range(kv_heads):
        span = slice(kh * group, (kh + 1) * group)
        q = all_q[:, span].reshape(total, HDIM)
        block = blk[:, :, kcols(kh)].reshape(sub_count * rows, HDIM)
        near = qkv[:, :, kcols(kh)].reshape(keys_q, HDIM)
        s0 = scores_of(q, block)
        s1 = jnp.where(
            seen, scores_of(q, near).reshape(shape4), masked_score
        ).reshape(total, keys_q)
        m = jnp.maximum(
            jnp.max(s0, axis=-1, keepdims=True), jnp.max(s1, axis=-1, keepdims=True)
        )
        acc = add_up(
            weights_of(s0, m), blk[:, :, vcols(kh)].reshape(sub_count * rows, HDIM)
        ) + add_up(weights_of(s1, m), qkv[:, :, vcols(kh)].reshape(keys_q, HDIM))
        sacc[:, span] = acc[:, :HDIM].astype(jnp.bfloat16).reshape(
            ctx_count, group, padded, HDIM
        )
        sums = acc[:, HDIM:]
        for z in range(ctx_count):
            for g in range(group):
                cut = slice((z * group + g) * padded, (z * group + g + 1) * padded)
                head = kh * group + g
                stats[z] = jnp.where(lane == head, m[cut], stats[z])
                stats[z] = jnp.where(lane == HDIM // 2 + head, sums[cut], stats[z])
    for z in range(ctx_count):
        sstat[z] = stats[z]

    def send_result(step, other, home):
        return pltpu.make_async_remote_copy(
            sacc.at[other], racc.at[home], r_send.at[other], r_recv.at[home],
            device_id={"ctx": other}, device_id_type=MESH,
        )

    def send_stat(step, other, home):
        return pltpu.make_async_remote_copy(
            sstat.at[other], rstat.at[home], t_send.at[other], t_recv.at[home],
            device_id={"ctx": other}, device_id_type=MESH,
        )

    for step in range(1, ctx_count):
        other = lax.rem(ctx + step, ctx_count)
        send_result(step, other, ctx).start()
        send_stat(step, other, ctx).start()
    racc[ctx] = sacc[ctx]
    rstat[ctx] = sstat[ctx]

    forward(2, ctx == 2)
    forward(3, ctx == 2)
    for i in range(CHUNKS):
        forward(i, ctx > 2)

    def finish(kh, t, acc):
        done = (acc[:, :HDIM] / acc[:, HDIM:]).astype(jnp.bfloat16)
        start = pl.multiple_of(t * TILE, TILE)
        for g in range(group):
            head = kh * group + g
            out_ref[pl.ds(start, TILE), head * HDIM:(head + 1) * HDIM] = done[
                g * TILE:(g + 1) * TILE
            ]

    @pl.when(ctx == 0)
    def _():
        @pl.loop(0, tiles)
        def _(t):
            for kh in range(kv_heads):
                finish(kh, t, acc1[kh, t])

    @pl.when(ctx > 0)
    def _():
        for i in range(CHUNKS):
            recv_pair(i).wait_recv()

        @pl.loop(0, tiles)
        def _(t):
            for kh in range(kv_heads):
                _, acc = merged(
                    kh, t,
                    anc[:, :, :, kcols(kh)].reshape(sub_count * rows, HDIM),
                    anc[:, :, :, vcols(kh)].reshape(sub_count * rows, HDIM),
                )
                finish(kh, t, acc)

    for step in range(1, ctx_count):
        other = lax.rem(ctx + step, ctx_count)
        send_result(step, ctx, other).wait_recv()
        send_stat(step, ctx, other).wait_recv()

    got = [rstat[z] for z in range(ctx_count)]
    top = functools.reduce(jnp.maximum, got)
    scaled = [jnp.exp2((one - top) * exponent_scale) for one in got]
    for h in range(q_heads):
        above = jnp.zeros((padded, HDIM), jnp.float32)
        under = jnp.zeros((padded, 1), jnp.float32)
        for z in range(ctx_count):
            w = scaled[z][:, h:h + 1]
            above = above + w * racc[z, h].astype(jnp.float32)
            under = under + w * got[z][:, HDIM // 2 + h:HDIM // 2 + h + 1]
        qout_ref[:, h * HDIM:(h + 1) * HDIM] = (above / under).astype(jnp.bfloat16)

    swap(blk, blk_sem, sub).wait_send()
    swap(qkv, qkv_sem, sub).wait_send()
    for step in range(1, ctx_count):
        other = lax.rem(ctx + step, ctx_count)
        send_query(step).wait_send()
        send_result(step, other, ctx).wait_send()
        send_stat(step, other, ctx).wait_send()

    @pl.when(ctx == 0)
    def _():
        for i in range(CHUNKS):
            send_first(i).wait_send()

    @pl.when(ctx > 0)
    def _():
        for i in range(CHUNKS):
            send_pair(i).wait_send()

    @pl.when((ctx > 0) & (ctx < ctx_count - 1))
    def _():
        for i in range(CHUNKS):
            send_on(i).wait_send()


def turns(positions):
    half = HDIM // 2
    inverse = rope_base ** (-(jnp.arange(half, dtype=jnp.float32) * 2.0 / HDIM))
    angles = positions.astype(jnp.float32)[:, None] * inverse[None, :]
    cosine = jnp.cos(angles)
    sine = jnp.sin(angles)
    return (
        jnp.concatenate([cosine, cosine], axis=1),
        jnp.concatenate([-sine, sine], axis=1),
    )


def shards(hidden, query_hidden, norm_gain, w_query, w_key, w_value):
    rows, width = hidden.shape
    query_rows = query_hidden.shape[0]
    padded = -(-query_rows // 16) * 16
    q_cols = w_query.shape[1]
    key_cols = w_key.shape[1]
    q_heads = q_cols // HDIM
    kv_heads = key_cols // HDIM
    group = q_heads // kv_heads
    tiles = rows // TILE
    ctx_count = lax.axis_size("ctx")
    sub_count = lax.axis_size("sub")
    ctx = lax.axis_index("ctx")
    sub = lax.axis_index("sub")
    if padded != query_rows:
        query_hidden = jnp.pad(query_hidden, ((0, padded - query_rows), (0, 0)))
    slot = ctx * sub_count + sub
    positions = jnp.concatenate(
        [
            slot * rows + jnp.arange(rows, dtype=jnp.int32),
            ctx_count * sub_count * rows
            + slot * query_rows
            + jnp.arange(padded, dtype=jnp.int32),
        ]
    )
    cosine, sine = turns(positions)
    wq_width = min(256, q_cols)
    bf16, f32 = jnp.bfloat16, jnp.float32
    dma = pltpu.SemaphoreType.DMA
    vmem = pl.BlockSpec(memory_space=pltpu.VMEM)
    hbm = pl.BlockSpec(memory_space=pl.ANY)
    out, qout = pl.pallas_call(
        functools.partial(kernel, (ctx_count, sub_count, query_rows)),
        out_shape=(
            jax.ShapeDtypeStruct((rows, q_cols), bf16),
            jax.ShapeDtypeStruct((padded, q_cols), bf16),
        ),
        in_specs=[hbm, hbm, vmem, vmem, vmem, hbm, hbm, hbm],
        out_specs=(vmem, vmem),
        scratch_shapes=[
            pltpu.VMEM((rows, width), bf16),
            pltpu.VMEM((padded, width), bf16),
            pltpu.VMEM((rows + padded, width), bf16),
            pltpu.VMEM((q_cols // wq_width, width, wq_width), bf16),
            pltpu.VMEM((width, key_cols), bf16),
            pltpu.VMEM((width, key_cols), bf16),
            pltpu.VMEM((q_heads, rows, HDIM), bf16),
            pltpu.VMEM((q_heads, padded, HDIM), bf16),
            pltpu.VMEM((ctx_count, q_heads, padded, HDIM), bf16),
            pltpu.VMEM((sub_count, rows, 2 * key_cols), bf16),
            pltpu.VMEM((sub_count, padded, 2 * key_cols), bf16),
            pltpu.VMEM((sub_count, CHUNKS, rows // CHUNKS, 2 * key_cols), bf16),
            pltpu.VMEM((kv_heads, tiles, group * TILE, 2 * HDIM), f32),
            pltpu.VMEM((kv_heads, tiles, group * TILE, HDIM), f32),
            pltpu.VMEM((ctx_count, q_heads, padded, HDIM), bf16),
            pltpu.VMEM((ctx_count, padded, HDIM), f32),
            pltpu.VMEM((ctx_count, q_heads, padded, HDIM), bf16),
            pltpu.VMEM((ctx_count, padded, HDIM), f32),
            dma((tiles,)), dma, dma, dma, dma((q_cols // wq_width,)),
            dma((2,)), dma((2,)),
            dma((CHUNKS,)), dma((CHUNKS,)), dma((CHUNKS,)), dma((CHUNKS,)),
            dma((ctx_count,)), dma((ctx_count,)), dma((ctx_count,)), dma((ctx_count,)),
            dma((ctx_count,)), dma((ctx_count,)),
        ],
        compiler_params=pltpu.CompilerParams(
            collective_id=0, has_side_effects=True, vmem_limit_bytes=58 * 1024 * 1024
        ),
    )(hidden, query_hidden, norm_gain.reshape(1, width), cosine, sine, w_query, w_key, w_value)
    return out, qout[:query_rows]


def solution(mesh):
    return jax.shard_map(
        shards,
        mesh=mesh,
        in_specs=(
            P(("grp", "ctx", "sub"), None),
            P(("grp", "ctx", "sub"), None),
            P(),
            P(None, "head"),
            P(None, "head"),
            P(None, "head"),
        ),
        out_specs=(P(("grp", "ctx", "sub"), "head"), P(("grp", "ctx", "sub"), "head")),
        check_vma=False,
    )
```

time: 194 us -> 70.6 us (0.36); the launches traced: 191 us -> 70.4 us
  Pallas kernels: 0 us -> 63.9 us
  matrix products: 61.5 us -> 0 us
  waiting for transfers between devices: 49.4 us -> 0 us
  blocking collectives: 28.7 us -> 0 us
  other arithmetic: 18.8 us -> 2.09 us
  between operations: 15.9 us -> 0.68 us
  local copies, waits for them, and re-layouts: 16.7 us -> 3.74 us
    pallas_call x0 -> x1, Pallas kernels: none -> 63.9 us  [shards(): pl.pallas_call(functools.partial(kernel, (ctx_count, sub_count, query_row...]
    reduce_scatter x1 -> x0, waiting for transfers between devices: 43.9 us -> none  [shards(): lax.psum_scatter((row_sums * factor[..., None]).astype(jnp.bfloat16), ('c...]
    dot_general x9 -> x0, matrix products: 40.9 us -> none  [the longest x2 15.6 us: project(): jnp.dot(normed, w_query, preferred_element_type=jnp.float32)]
    sub x1 -> x0, matrix products: 20.6 us -> none  [attend(): weights = jnp.where(mask_full, jnp.exp(scores - maxima[..., None]), 0.0)]
    all_gather x1 -> x0, blocking collectives: 15.4 us -> none  [shards(): lax.all_gather(own_queries, ('ctx', 'sub'), axis=0, tiled=True)]
    pmax x1 -> x0, blocking collectives: 13.3 us -> none  [shards(): global_max = lax.pmax(row_maxima, ('ctx', 'sub'))]
    reduce_sum x3 -> x0, other arithmetic: 6.76 us -> none  [the longest x2 3.39 us: normalize(): meansq = jnp.mean(widened * widened, axis=-1, keepdims=True) + norm_eps]
    unnamed x5 -> x0, waiting for transfers between devices: 5.48 us -> none
  transfers between devices with their start and end apart: 4 -> 0, of which waited for: 2 -> 0; matrix products, arithmetic and copies ran while one was open for 21% -> 0% of each run, Pallas kernels for 0% -> 0%
where the time goes in v1:
time: 70.6 us; the launch traced here: 70.4 us
  Pallas kernels  63.9 us (91%)
  local copies, waits for them, and re-layouts  3.74 us (5%)
  other arithmetic  2.09 us (3%)
    pallas_call x1, Pallas kernels, shards(): pl.pallas_call(functools.partial(kernel, (ctx_count, sub_count, query_row...  63.9 us
    unnamed x2, local copies, waits for them, and re-layouts  3.74 us

profile of v1, /device:TPU:31, one launch (start us, length us, event | category | flops | bytes accessed | tf_op | source)
XLA Modules:
  0.0 70.4 jit_solution(5104114713483146062)
XLA Ops:
  0.7 1.0 %fusion = (f32[544,64]{1,0:T(8,128)S(1)}, f32[544,64]{1,0:T(8,128)S(1)}, f32[544,64]{1,0:T(8,128)S(1)}) fusion(f32[64]{0:T(128)S(1)} %negate_power_fusion, f32[544]{0:T(1024)S(1)} %add_convert_fusion), kind=kLoop, calls=%fused_computation.4 | loop fusion | flops 69632 | bytes 420224 | tf_op jit(solution)/shard_map/neg | solution.py:411
  1.7 1.0 %pad_maximum_fusion = (f32[544,128]{1,0:T(8,128)}, f32[544,128]{1,0:T(8,128)}) fusion(f32[544,64]{1,0:T(8,128)S(1)} %get-tuple-element.4, f32[544,64]{1,0:T(8,128)S(1)} %get-tuple-element.3, f32[544,64]{1,0:T(8,128)S(1)} %get-tuple-element.2), kind=kLoop, calls=%fused_computation.2 | loop fusion | flops 139264 | bytes 974848 | tf_op jit(solution)/shard_map/concatenate | solution.py:410
  2.8 63.9 %shard_map.77 = (bf16[512,1024]{1,0:T(8,128)(2,1)}, bf16[32,1024]{1,0:T(8,128)(2,1)}) custom-call(bf16[512,4096]{1,0:T(8,128)(2,1)} %hidden_hbm.1, bf16[32,4096]{1,0:T(8,128)(2,1)} %qhidden_hbm.1, f32[1,4096]{1,0:T(1,128)} %bitcast.1, f32[544,128]{1,0:T(8,128)} %get-tuple-element.5.cos_ref, f32[544,128]{1,0:T(8,128)} %get-tuple-element.6.sin_ref, ...), custom_call_target="tpu_custom_call" | custom-call | tf_op jit(solution)/shard_map/pallas_call | solution.py:446
  66.7 2.3 %copy.10 = bf16[512,1024]{1,0:T(8,128)(2,1)} copy(bf16[512,1024]{1,0:T(8,128)(2,1)} %get-tuple-element.9) | data formatting | bytes 2097152
  68.9 1.5 %copy.11 = bf16[32,1024]{1,0:T(8,128)(2,1)} copy(bf16[32,1024]{1,0:T(8,128)(2,1)} %get-tuple-element.10) | data formatting | bytes 131072
  (4 shorter events, 0.0 us)

commit v2 on v1

--- a/solution.py
+++ b/solution.py
@@ -10,7 +10,14 @@
 
 HDIM = 128
 TILE = 128
-CHUNKS = 4
+CHUNKS = 8
+
+LATEST = 3
+SCHEDULE = {
+    1: ["q1", "q2", "q3", "q3", "d1", "d3", "peer", "peer"],
+    2: ["q3", "d1", "d3", "peer", "peer", "peer", "near0", "near1"],
+    LATEST: ["peer", "peer", "peer", "near0", "near0", "near1", "near1", "near1"],
+}
 
 rope_base = 500000.0
 norm_eps = 1e-05
@@ -23,10 +30,10 @@
 
 def kernel(
     sizes,
-    hidden_hbm, qhidden_hbm, gain_ref, cos_ref, sin_ref, wq_hbm, wk_hbm, wv_hbm,
+    hidden_hbm, qhidden_hbm, gain_ref, cosine_ref, sine_ref, wq_hbm, wk_hbm, wv_hbm,
     out_ref, qout_ref,
     hid, qhid, normed, wq, wk, wv, heads_q, own_q, all_q, blk, qkv, anc,
-    acc1, max1, sacc, sstat, racc, rstat,
+    acc1, max1, sacc, sstat, racc, rstat, cos_ref, sin_ref,
     load_sem, qload_sem, wk_sem, wv_sem, wq_sem,
     blk_sem, qkv_sem, chain_send, chain_recv, pair_send, pair_recv,
     q_send, q_recv, r_send, r_recv, t_send, t_recv,
@@ -73,17 +80,20 @@
         pl.semaphore_signal(barrier, inc=1, device_id={"ctx": other}, device_id_type=MESH)
     pl.semaphore_signal(barrier, inc=1, device_id={"sub": peer}, device_id_type=MESH)
 
+    cos_ref[...] = jnp.concatenate([cosine_ref[...], cosine_ref[...]], axis=1)
+    sin_ref[...] = jnp.concatenate([-sine_ref[...], sine_ref[...]], axis=1)
     gain = gain_ref[...]
 
     def norm_rows(source, start, target, count):
         wide = source[pl.ds(start, count), :].astype(jnp.float32)
         meansq = jnp.mean(wide * wide, axis=-1, keepdims=True) + norm_eps
+        wide = source[pl.ds(start, count), :].astype(jnp.float32)
         normed[pl.ds(target, count), :] = (wide * lax.rsqrt(meansq) * gain).astype(jnp.bfloat16)
 
     for i in range(tiles):
         load_rows(i).wait()
 
-        @pl.loop(0, TILE // 16)
+        @pl.loop(0, TILE // 16, unroll=2)
         def _(b):
             start = pl.multiple_of(i * TILE + b * 16, 16)
             norm_rows(hid, start, start, 16)
@@ -155,16 +165,23 @@
     swap(blk, blk_sem, sub).start()
     swap(qkv, qkv_sem, sub).start()
 
-    def forward(i, which):
-        @pl.when(which)
+    def forward(i):
+        send_on(i).wait_recv()
+
+        @pl.when(ctx < ctx_count - 1)
         def _():
-            send_on(i).wait_recv()
-
-            @pl.when(ctx < ctx_count - 1)
-            def _():
-                send_on(i).start()
-
-            send_pair(i).start()
+            send_on(i).start()
+
+        send_pair(i).start()
+
+    def point(name):
+        for place, plan in SCHEDULE.items():
+            due = [i for i in range(CHUNKS) if plan[i] == name]
+            if due:
+                @pl.when(ctx >= place if place == LATEST else ctx == place)
+                def _():
+                    for i in due:
+                        forward(i)
 
     per_tile = wq_width // HDIM
     for j in range(wq_tiles):
@@ -175,6 +192,9 @@
             turned = rotated(made, t)
             heads_q[j * per_tile + t] = turned[:rows]
             own_q[j * per_tile + t] = turned[rows:]
+        for at in range(3):
+            if at * wq_tiles // 4 == j:
+                point(f"q{at}")
 
     def send_query(step):
         other = lax.rem(ctx + step, ctx_count)
@@ -194,7 +214,7 @@
         send_query(step).start()
     all_q[ctx] = own_q[...]
 
-    forward(0, ctx == 1)
+    point("q3")
 
     def scores_of(q, k):
         return lax.dot_general(q, k, NT_DIMS, preferred_element_type=jnp.float32)
@@ -231,11 +251,9 @@
             m = jnp.max(s, axis=-1, keepdims=True)
             acc1[kh, t] = add_up(weights_of(s, m), blk[sub, :span, vcols(kh)])
             max1[kh, t] = jnp.broadcast_to(m, (group * TILE, HDIM))
-        if t == tiles // 2 - 1:
-            forward(1, ctx == 1)
-
-    forward(2, ctx == 1)
-    forward(0, ctx == 2)
+        for at in range(4):
+            if at * tiles // 4 == t:
+                point(f"d{at}")
 
     def merged(kh, t, k, v):
         s = scores_of(tile_q(kh, pl.multiple_of(t * TILE, TILE)), k)
@@ -257,8 +275,7 @@
                 acc1[kh, t] = acc
                 max1[kh, t] = m
 
-    forward(3, ctx == 1)
-    forward(1, ctx == 2)
+    point("peer")
 
     for step in range(1, ctx_count):
         recv_query(step).wait_recv()
@@ -301,6 +318,8 @@
                 head = kh * group + g
                 stats[z] = jnp.where(lane == head, m[cut], stats[z])
                 stats[z] = jnp.where(lane == HDIM // 2 + head, sums[cut], stats[z])
+        if kh == 0:
+            point("near0")
     for z in range(ctx_count):
         sstat[z] = stats[z]
 
@@ -323,10 +342,7 @@
     racc[ctx] = sacc[ctx]
     rstat[ctx] = sstat[ctx]
 
-    forward(2, ctx == 2)
-    forward(3, ctx == 2)
-    for i in range(CHUNKS):
-        forward(i, ctx > 2)
+    point("near1")
 
     def finish(kh, t, acc):
         done = (acc[:, :HDIM] / acc[:, HDIM:]).astype(jnp.bfloat16)
@@ -406,10 +422,7 @@
     angles = positions.astype(jnp.float32)[:, None] * inverse[None, :]
     cosine = jnp.cos(angles)
     sine = jnp.sin(angles)
-    return (
-        jnp.concatenate([cosine, cosine], axis=1),
-        jnp.concatenate([-sine, sine], axis=1),
-    )
+    return cosine, sine
 
 
 def shards(hidden, query_hidden, norm_gain, w_query, w_key, w_value):
@@ -446,8 +459,8 @@
     out, qout = pl.pallas_call(
         functools.partial(kernel, (ctx_count, sub_count, query_rows)),
         out_shape=(
-            jax.ShapeDtypeStruct((rows, q_cols), bf16),
-            jax.ShapeDtypeStruct((padded, q_cols), bf16),
+            pltpu.VMEM((rows, q_cols), bf16),
+            pltpu.VMEM((padded, q_cols), bf16),
         ),
         in_specs=[hbm, hbm, vmem, vmem, vmem, hbm, hbm, hbm],
         out_specs=(vmem, vmem),
@@ -470,6 +483,8 @@
             pltpu.VMEM((ctx_count, padded, HDIM), f32),
             pltpu.VMEM((ctx_count, q_heads, padded, HDIM), bf16),
             pltpu.VMEM((ctx_count, padded, HDIM), f32),
+            pltpu.VMEM((rows + padded, HDIM), f32),
+            pltpu.VMEM((rows + padded, HDIM), f32),
             dma((tiles,)), dma, dma, dma, dma((q_cols // wq_width,)),
             dma((2,)), dma((2,)),
             dma((CHUNKS,)), dma((CHUNKS,)), dma((CHUNKS,)), dma((CHUNKS,)),

time: 70.6 us -> 62.7 us (0.89); the launches traced: 70.4 us -> 61.6 us
  Pallas kernels: 63.9 us -> 57.5 us
  local copies, waits for them, and re-layouts: 3.74 us -> 1.6 us
    pallas_call x1, Pallas kernels: 63.9 us -> 57.5 us  [shards(): pl.pallas_call(functools.partial(kernel, (ctx_count, sub_count, query_row...]
    unnamed x2, local copies, waits for them, and re-layouts: 3.74 us -> 1.6 us
    sin x0 -> x1, other arithmetic: none -> 1.86 us  [turns(): sine = jnp.sin(angles)]
    neg x1 -> x0, other arithmetic: 1.05 us -> none  [turns(): -sine]
    concatenate x1 -> x0, other arithmetic: 1.02 us -> none  [turns(): jnp.concatenate([cosine, cosine], axis=1)]
where the time goes in v2:
time: 62.7 us; the launch traced here: 61.6 us
  Pallas kernels  57.5 us (92%)
  other arithmetic  1.89 us (3%)
  local copies, waits for them, and re-layouts  1.6 us (3%)
  between operations  0.67 us (1%)
    pallas_call x1, Pallas kernels, shards(): pl.pallas_call(functools.partial(kernel, (ctx_count, sub_count, query_row...  57.5 us
    sin x1, other arithmetic, turns(): sine = jnp.sin(angles)  1.86 us
    unnamed x2, local copies, waits for them, and re-layouts  1.6 us

profile of v2, /device:TPU:31, one launch (start us, length us, event | category | flops | bytes accessed | tf_op | source)
XLA Modules:
  0.0 61.6 jit_solution(14134265957230596896)
XLA Ops:
  0.7 1.9 %multiply_sine_fusion = (f32[544,64]{1,0:T(8,128)}, f32[544,64]{1,0:T(8,128)}) fusion(f32[64]{0:T(128)S(1)} %negate_power_fusion, f32[544]{0:T(1024)S(1)} %add_convert_fusion), kind=kLoop, calls=%fused_computation | loop fusion | flops 34816 | bytes 280960 | tf_op jit(solution)/shard_map/sin | solution.py:424
  2.6 57.5 %shard_map.77 = (bf16[512,1024]{1,0:T(8,128)(2,1)S(1)}, bf16[32,1024]{1,0:T(8,128)(2,1)S(1)}) custom-call(bf16[512,4096]{1,0:T(8,128)(2,1)} %hidden_hbm.1, bf16[32,4096]{1,0:T(8,128)(2,1)} %qhidden_hbm.1, f32[1,4096]{1,0:T(1,128)} %bitcast.1, f32[544,64]{1,0:T(8,128)} %get-tuple-element.3.cosine_ref, f32[544,64]{1,0:T(8,128)} %get-tuple-element.2.sine_ref, ...), custom_call_target="tpu_custom_call" | custom-call | tf_op jit(solution)/shard_map/pallas_call | solution.py:459
  60.0 1.0 %copy.10 = bf16[512,1024]{1,0:T(8,128)(2,1)} copy(bf16[512,1024]{1,0:T(8,128)(2,1)S(1)} %get-tuple-element.4) | data formatting | bytes 2097152
  61.0 0.6 %copy.11 = bf16[32,1024]{1,0:T(8,128)(2,1)} copy(bf16[32,1024]{1,0:T(8,128)(2,1)S(1)} %get-tuple-element.5) | data formatting | bytes 131072
  (4 shorter events, 0.0 us)

commit v3 on v2

--- a/solution.py
+++ b/solution.py
@@ -14,9 +14,9 @@
 
 LATEST = 3
 SCHEDULE = {
-    1: ["q1", "q2", "q3", "q3", "d1", "d3", "peer", "peer"],
-    2: ["q3", "d1", "d3", "peer", "peer", "peer", "near0", "near1"],
-    LATEST: ["peer", "peer", "peer", "near0", "near0", "near1", "near1", "near1"],
+    1: ["q1", "q1", "q2", "q2", "q3", "q3", "d1", "d3"],
+    2: ["q3", "q3", "d1", "d2", "d3", "d3", "peer", "peer"],
+    LATEST: ["peer", "peer", "near0", "near0", "half", "half", "half", "half"],
 }
 
 rope_base = 500000.0
@@ -362,17 +362,34 @@
 
     @pl.when(ctx > 0)
     def _():
-        for i in range(CHUNKS):
+        half = CHUNKS // 2
+
+        def anchor_part(first, kh, t):
+            keys_in = sub_count * half * part
+            return merged(
+                kh, t,
+                anc[:, first:first + half, :, kcols(kh)].reshape(keys_in, HDIM),
+                anc[:, first:first + half, :, vcols(kh)].reshape(keys_in, HDIM),
+            )
+
+        for i in range(half):
             recv_pair(i).wait_recv()
 
         @pl.loop(0, tiles)
         def _(t):
             for kh in range(kv_heads):
-                _, acc = merged(
-                    kh, t,
-                    anc[:, :, :, kcols(kh)].reshape(sub_count * rows, HDIM),
-                    anc[:, :, :, vcols(kh)].reshape(sub_count * rows, HDIM),
-                )
+                m, acc = anchor_part(0, kh, t)
+                acc1[kh, t] = acc
+                max1[kh, t] = m
+
+        point("half")
+        for i in range(half, CHUNKS):
+            recv_pair(i).wait_recv()
+
+        @pl.loop(0, tiles)
+        def _(t):
+            for kh in range(kv_heads):
+                _, acc = anchor_part(half, kh, t)
                 finish(kh, t, acc)
 
     for step in range(1, ctx_count):

time: 62.7 us -> 58 us (0.925)
  the two profiles are of different devices: /device:TPU:31 before, /device:TPU:17 now
where the time goes in v3:
time: 58 us; the launch traced here: 57.8 us
  Pallas kernels  53.7 us (93%)
  other arithmetic  1.89 us (3%)
  local copies, waits for them, and re-layouts  1.6 us (3%)
  between operations  0.67 us (1%)
    pallas_call x1, Pallas kernels, shards(): pl.pallas_call(functools.partial(kernel, (ctx_count, sub_count, query_row...  53.7 us
    sin x1, other arithmetic, turns(): sine = jnp.sin(angles)  1.86 us
    unnamed x2, local copies, waits for them, and re-layouts  1.6 us

profile of v3, /device:TPU:17, one launch (start us, length us, event | category | flops | bytes accessed | tf_op | source)
XLA Modules:
  0.0 57.8 jit_solution(9723245350826351994)
XLA Ops:
  0.7 1.9 %multiply_sine_fusion = (f32[544,64]{1,0:T(8,128)}, f32[544,64]{1,0:T(8,128)}) fusion(f32[64]{0:T(128)S(1)} %negate_power_fusion, f32[544]{0:T(1024)S(1)} %add_convert_fusion), kind=kLoop, calls=%fused_computation | loop fusion | flops 34816 | bytes 280960 | tf_op jit(solution)/shard_map/sin | solution.py:441
  2.6 53.7 %shard_map.77 = (bf16[512,1024]{1,0:T(8,128)(2,1)S(1)}, bf16[32,1024]{1,0:T(8,128)(2,1)S(1)}) custom-call(bf16[512,4096]{1,0:T(8,128)(2,1)} %hidden_hbm.1, bf16[32,4096]{1,0:T(8,128)(2,1)} %qhidden_hbm.1, f32[1,4096]{1,0:T(1,128)} %bitcast.1, f32[544,64]{1,0:T(8,128)} %get-tuple-element.3.cosine_ref, f32[544,64]{1,0:T(8,128)} %get-tuple-element.2.sine_ref, ...), custom_call_target="tpu_custom_call" | custom-call | tf_op jit(solution)/shard_map/pallas_call | solution.py:476
  56.2 1.0 %copy.10 = bf16[512,1024]{1,0:T(8,128)(2,1)} copy(bf16[512,1024]{1,0:T(8,128)(2,1)S(1)} %get-tuple-element.4) | data formatting | bytes 2097152
  57.2 0.6 %copy.11 = bf16[32,1024]{1,0:T(8,128)(2,1)} copy(bf16[32,1024]{1,0:T(8,128)(2,1)S(1)} %get-tuple-element.5) | data formatting | bytes 131072
  (4 shorter events, 0.0 us)
